TPU v7x, 32 devices: a whole 2x2x4 slice. The times are simulated.
32 devices in a mesh: ctx: 16 (over z, x, core), tp: 2 (over y).
Axes of the slice: x: 2, y: 2, z: 4, core: 2. Of those that a mesh axis runs over, the one named last changes fastest.
Arguments:
- queries: bfloat16 [2048, 4096], P('ctx', 'tp'), may hold values from -5 to 5
- keys: bfloat16 [2048, 1024], P('ctx', 'tp'), may hold values from -5 to 5
- values: bfloat16 [2048, 1024], P('ctx', 'tp'), may hold values from -6 to 6
- out_grad: bfloat16 [2048, 4096], P('ctx', 'tp'), may hold values from -6 to 6
- features: bfloat16 [2048, 4096], P('ctx'), may hold values from -6 to 6
- segment_ids: int32 [2048], replicated, may hold values from 0 to 15, never falling along the last dimension, each value on 1 to 1536 neighbouring positions
Outputs:
- query_grads: bfloat16 [2048, 4096], P('ctx', 'tp')
- weight_grad: float32 [4096, 1024], P('tp')
Inputs may be any that keep to these rules, and one draw needn't show every extreme that they name: `segment_ids`: never falling along the sequence; each document has 1 to 1536 tokens and one has exactly 1536.
All inputs are finite; a program needn't handle non-finite values.
Results may differ from a plain program's by a relative error of at most 0.024.
Values may be sent and summed in bfloat16 or wider, within the bound.
A program may use at most 64 MiB of HBM per device.

v0:
```python
import math

import jax
import jax.numpy as jnp
from jax import lax
from jax.sharding import PartitionSpec as P

HD = 128


def per_device(queries, keys, values, out_grad, features, segment_ids):
    rows = queries.shape[0]
    heads_q = queries.shape[1] // HD
    heads_kv = keys.shape[1] // HD
    group = heads_q // heads_kv
    tokens = segment_ids.shape[0]
    width = math.gcd(tokens, 1024)
    scale = HD ** (-0.5)
    first = lax.axis_index("ctx") * rows
    gathered = (
        lax.all_gather(keys, "ctx", axis=0, tiled=True),
        lax.all_gather(values, "ctx", axis=0, tiled=True),
    )
    key_all = gathered[0].reshape(tokens, heads_kv, HD)
    value_all = gathered[1].reshape(tokens, heads_kv, HD)
    query_heads = queries.reshape(rows, heads_kv, group, HD)
    grad_heads = out_grad.reshape(rows, heads_kv, group, HD)
    seg_own = lax.dynamic_slice_in_dim(segment_ids, first, rows, 0)
    pos_own = first + jnp.arange(rows, dtype=jnp.int32)
    last_row = first + rows - 1
    seg_first = seg_own[0]

    def active(start, count):
        seg_end = lax.dynamic_index_in_dim(segment_ids, start + count - 1, 0, keepdims=False)
        return (start <= last_row) & (seg_end >= seg_first)

    def masked_scores(start, count):
        key_block = lax.dynamic_slice_in_dim(key_all, start, count, 0)
        seg_block = lax.dynamic_slice_in_dim(segment_ids, start, count, 0)
        pos_block = start + jnp.arange(count, dtype=jnp.int32)
        allowed = (pos_block[None, :] <= pos_own[:, None]) & (
            seg_block[None, :] == seg_own[:, None]
        )
        scores = (
            jnp.einsum("qngd,knd->ngqk", query_heads, key_block, preferred_element_type=jnp.float32)
            * scale
        )
        return (jnp.where(allowed, scores, -1e30), allowed)

    starts = jnp.arange(tokens // width, dtype=jnp.int32) * width

    def forward_step(carry, start):

        def forward_work(state):
            top, total, accum = state
            scores, allowed = masked_scores(start, width)
            top_new = jnp.maximum(top, jnp.max(scores, axis=-1))
            factor = jnp.exp(top - top_new)
            weights = jnp.where(allowed, jnp.exp(scores - top_new[..., None]), 0.0)
            value_block = lax.dynamic_slice_in_dim(value_all, start, width, 0)
            update = jnp.einsum(
                "ngqk,knd->ngqd",
                weights.astype(jnp.bfloat16),
                value_block,
                preferred_element_type=jnp.float32,
            )
            accum = accum * factor[..., None] + update
            total = total * factor + jnp.sum(weights, axis=-1)
            return (top_new, total, accum)

        def keep(state):
            return state

        return (lax.cond(active(start, width), forward_work, keep, carry), None)

    initial = (
        jnp.full((heads_kv, group, rows), -1e30, jnp.float32),
        jnp.zeros((heads_kv, group, rows), jnp.float32),
        jnp.zeros((heads_kv, group, rows, HD), jnp.float32),
    )
    (top, total, accum), _ = lax.scan(forward_step, initial, starts)
    attended = (accum / total[..., None]).astype(jnp.bfloat16)
    log_total = top + jnp.log(total)
    delta = jnp.einsum("qngd,ngqd->ngq", grad_heads, attended, preferred_element_type=jnp.float32)

    def probabilities(start, count):
        scores, allowed = masked_scores(start, count)
        return jnp.where(allowed, jnp.exp(scores - log_total[..., None]), 0.0)

    def query_update(carry, start, probs):
        key_block = lax.dynamic_slice_in_dim(key_all, start, width, 0)
        value_block = lax.dynamic_slice_in_dim(value_all, start, width, 0)
        dprob = jnp.einsum(
            "qngd,knd->ngqk", grad_heads, value_block, preferred_element_type=jnp.float32
        )
        dscore = probs * (dprob - delta[..., None])
        return carry + jnp.einsum(
            "ngqk,knd->qngd",
            dscore.astype(jnp.bfloat16),
            key_block,
            preferred_element_type=jnp.float32,
        )

    def value_part(probs, count):
        part = jnp.einsum(
            "ngqk,qngd->knd",
            probs.astype(jnp.bfloat16),
            grad_heads,
            preferred_element_type=jnp.float32,
        )
        return part.reshape(count, heads_kv * HD)

    zero_grad = jnp.zeros((rows, heads_kv, group, HD), jnp.float32)

    def after_step(carry, start):

        def after_work(state):
            probs = probabilities(start, width)
            return (query_update(state, start, probs), value_part(probs, width))

        def rest(state):
            return (state, jnp.zeros((width, heads_kv * HD), jnp.float32))

        return lax.cond(active(start, width), after_work, rest, carry)

    query_accum, blocks = lax.scan(after_step, zero_grad, starts)
    value_grad = lax.psum_scatter(
        blocks.reshape(tokens, heads_kv * HD), "ctx", scatter_dimension=0, tiled=True
    )
    query_grads = (query_accum * scale).astype(jnp.bfloat16).reshape(rows, heads_q * HD)
    value_b = value_grad.astype(jnp.bfloat16)
    factor_tokens = 1.0 / math.sqrt(tokens)
    contract = (((0,), (0,)), ((), ()))
    own_term = lax.dot_general(features, value_b, contract, preferred_element_type=jnp.float32)
    summed = lax.psum(own_term, "ctx")
    weight_grad = (
        lax.all_to_all(
            summed.astype(jnp.bfloat16), "tp", split_axis=0, concat_axis=1, tiled=True
        ).astype(summed.dtype)
        * factor_tokens
    )
    return (query_grads, weight_grad)


def solution(mesh):
    placed = (P("ctx", "tp"), P("ctx", "tp"), P("ctx", "tp"), P("ctx", "tp"), P("ctx", None), P())
    return jax.shard_map(
        per_device,
        mesh=mesh,
        in_specs=placed,
        out_specs=(P("ctx", "tp"), P("tp", None)),
        check_vma=False,
    )
```

profile of v0, /device:TPU:17, one launch (start us, length us, event | category | flops | bytes accessed | tf_op | source)
XLA Modules:
  0.0 535.4 jit_solution(12770206614781067422)
XLA Ops:
  7.2 1.7 copy.52
  9.1 1.7 copy.54
  10.8 2.1 copy.58
  12.9 1.3 copy.53
  14.2 1.0 copy.60
  15.2 0.8 dynamic_slice.60
  16.0 36.4 %all-gather.3.cloned.1.call-done = bf16[2048,512]{0,1:T(8,128)(2,1)} async-done(((bf16[128,512]{0,1:T(8,128)(2,1)}), bf16[2048,512]{0,1:T(8,128)(2,1)}) %all-gather.3.cloned.1.call-update) | async-done | bytes 2097168 | tf_op jit(solution)/shard_map/all_gather | solution.py:21
  52.3 3.9 copy.59
  56.3 38.4 %all-gather.5.cloned.1.call-done = bf16[2048,512]{0,1:T(8,128)(2,1)} async-done(((bf16[128,512]{0,1:T(8,128)(2,1)}), bf16[2048,512]{0,1:T(8,128)(2,1)}) %all-gather.5.cloned.1.call-update) | async-done | bytes 2097168 | tf_op jit(solution)/shard_map/all_gather | solution.py:22
  94.6 4.0 copy.57
  98.7 30.1 %while.39 = (s32[]{:T(128)}, f32[4,4,128]{2,1,0:T(4,128)S(1)}, f32[4,4,128]{2,1,0:T(4,128)S(1)}, f32[4,4,128,128]{3,2,1,0:T(8,128)S(1)}, s32[2]{0:T(128)S(1)}, /...) while((s32[]{:T(128)}, f32[4,4,128]{2,1,0:T(4,128)S(1)}, ...), condition=%wide.region_5.6_spmd.clone, body=%wide.region_0.5_spmd.clone.sunk | while | flops 1101927552 | bytes 38951908 | solution.py:81
  102.5 11.2 %conditional.6 = ((f32[4,4,128]{2,1,0:T(4,128)S(1)}, f32[4,4,128]{2,1,0:T(4,128)S(1)}, f32[4,4,128,128]{3,2,1,0:T(8,128)S(1)})) conditional(s32[]{:T(128)} %convert_element_type.72, (f32[4,4,128]{2,1,0:T(4,128)S(1)}, f32[4,4,128]{2,1,0:T(4,128)S(1)}, f32[4,4,128,128]{3,2,1,0:T(8,128)S(1)}) %tuple.113, (s32[]{:T(128)}, s32[]{:T(128)}, ...), branch_computations={%region_1.1_spmd, %region_2.4_spmd} | conditional | flops 1101927552 | bytes 38951024 | solution.py:74
  105.6 2.9 fusion.4
  108.5 2.0 fusion.6
  110.6 3.2 fusion.10
  117.5 11.2 %conditional.6 = ((f32[4,4,128]{2,1,0:T(4,128)S(1)}, f32[4,4,128]{2,1,0:T(4,128)S(1)}, f32[4,4,128,128]{3,2,1,0:T(8,128)S(1)})) conditional(s32[]{:T(128)} %convert_element_type.72, (f32[4,4,128]{2,1,0:T(4,128)S(1)}, f32[4,4,128]{2,1,0:T(4,128)S(1)}, f32[4,4,128,128]{3,2,1,0:T(8,128)S(1)}) %tuple.113, (s32[]{:T(128)}, s32[]{:T(128)}, ...), branch_computations={%region_1.1_spmd, %region_2.4_spmd} | conditional | flops 1101927552 | bytes 38951024 | solution.py:74
  120.6 2.9 fusion.4
  123.6 2.0 fusion.6
  125.6 3.2 fusion.10
  129.5 1.2 multiply_reduce_fusion
  130.7 1.1 broadcast_in_dim.59
  131.8 64.1 %while.40 = (s32[]{:T(128)}, f32[128,4,4,128]{0,3,2,1:T(8,128)}, f32[2,1024,512]{2,1,0:T(8,128)}, s32[2]{0:T(128)S(1)}, s32[]{:T(128)}, /*index=5*/s32[2048]{0:T...) while((s32[]{:T(128)}, f32[128,4,4,128]{0,3,2,1:T(8,128)}, ...), condition=%wide.region_9.10_spmd.clone, body=%wide.region_6.9_spmd.clone.sunk | while | flops 2173305856 | bytes 53395444 | solution.py:126
  131.8 0.6 dynamic_slice.94
  135.6 23.5 %conditional.7 = (f32[128,4,4,128]{0,3,2,1:T(8,128)}, f32[1,1024,512]{1,2,0:T(8,128)S(1)}) conditional(s32[]{:T(128)} %convert_element_type.73, f32[128,4,4,128]{0,3,2,1:T(8,128)} %get-tuple-element.1156, (s32[]{:T(128)}, bf16[2048,4,128]{2,0,1:T(8,128)(2,1)}, s32[]{:T(128)}, s32[2048]{0:T(1024)S(1)}, s32[128]{0:T(128)S(1)}, ...), branch_computations={%region_7.7_spmd, %region_8.8_spmd} | conditional | flops 2173305856 | bytes 36617312 | solution.py:124
  138.7 6.0 %fusion.43 = f32[4,1024,128,4]{2,1,3,0:T(8,128)} fusion(bf16[128,4,4,128]{3,0,2,1:T(8,128)(2,1)} %get-tuple-element.624, bf16[2048,4,128]{2,0,1:T(8,128)(2,1)} %get-tuple-element.619, s32[]{:T(128)S(6)} %select_n.41), kind=kOutput, calls=%fused_computation.40 | convolution fusion | flops 536870912 | bytes 9961476 | tf_op jit(solution)/shard_map/while/body/eval_jaxpr/cond/branch_1_fun/qngd,knd->ngqk/dot_general | solution.py:45
  144.7 8.7 %fusion.40 = f32[128,4,4,128]{0,3,2,1:T(8,128)} fusion(f32[128,4,4,128]{0,3,2,1:T(8,128)} %get-tuple-element.618, f32[4,1024,128,4]{2,1,3,0:T(8,128)} %fusion.43, f32[4,4,128]{2,1,0:T(4,128)S(1)} %get-tuple-element.628, f32[4,4,128]{2,1,0:T(4,128)S(1)} %get-tuple-element.625, pred[128,1024]{0,1:T(8,128)(4,1)S(1)} %compare_and_fusion.1, ...), kind=kOutput, calls=%fused_computation.39 | convolution fusion | flops 1088684032 | bytes 13255680 | tf_op jit(solution)/shard_map/while/body/eval_jaxpr/cond/branch_1_fun/ngqk,knd->qngd/dot_general | solution.py:97
  153.4 5.6 %fusion.29 = f32[4,1024,128,1]{1,2,3,0:T(8,128)S(1)} fusion(bf16[128,4,4,128]{0,3,2,1:T(8,128)(2,1)} %get-tuple-element.627, f32[4,1024,128,4]{2,1,3,0:T(8,128)} %fusion.43, f32[4,4,128]{2,1,0:T(4,128)S(1)} %get-tuple-element.625, pred[128,1024]{0,1:T(8,128)(4,1)S(1)} %compare_and_fusion.1), kind=kOutput, calls=%fused_computation.33 | convolution fusion | flops 547356672 | bytes 11149312 | tf_op jit(solution)/shard_map/while/body/eval_jaxpr/cond/branch_1_fun/ngqk,qngd->knd/dot_general | solution.py:105
  159.1 1.3 copy-done.1
  160.4 1.9 copy.91
  162.3 1.5 constant_dynamic-update-slice_fusion.2
  163.8 0.6 dynamic_slice.94
  167.6 23.5 %conditional.7 = (f32[128,4,4,128]{0,3,2,1:T(8,128)}, f32[1,1024,512]{1,2,0:T(8,128)S(1)}) conditional(s32[]{:T(128)} %convert_element_type.73, f32[128,4,4,128]{0,3,2,1:T(8,128)} %get-tuple-element.1156, (s32[]{:T(128)}, bf16[2048,4,128]{2,0,1:T(8,128)(2,1)}, s32[]{:T(128)}, s32[2048]{0:T(1024)S(1)}, s32[128]{0:T(128)S(1)}, ...), branch_computations={%region_7.7_spmd, %region_8.8_spmd} | conditional | flops 2173305856 | bytes 36617312 | solution.py:124
  170.7 6.0 %fusion.43 = f32[4,1024,128,4]{2,1,3,0:T(8,128)} fusion(bf16[128,4,4,128]{3,0,2,1:T(8,128)(2,1)} %get-tuple-element.624, bf16[2048,4,128]{2,0,1:T(8,128)(2,1)} %get-tuple-element.619, s32[]{:T(128)S(6)} %select_n.41), kind=kOutput, calls=%fused_computation.40 | convolution fusion | flops 536870912 | bytes 9961476 | tf_op jit(solution)/shard_map/while/body/eval_jaxpr/cond/branch_1_fun/qngd,knd->ngqk/dot_general | solution.py:45
  176.7 8.7 %fusion.40 = f32[128,4,4,128]{0,3,2,1:T(8,128)} fusion(f32[128,4,4,128]{0,3,2,1:T(8,128)} %get-tuple-element.618, f32[4,1024,128,4]{2,1,3,0:T(8,128)} %fusion.43, f32[4,4,128]{2,1,0:T(4,128)S(1)} %get-tuple-element.628, f32[4,4,128]{2,1,0:T(4,128)S(1)} %get-tuple-element.625, pred[128,1024]{0,1:T(8,128)(4,1)S(1)} %compare_and_fusion.1, ...), kind=kOutput, calls=%fused_computation.39 | convolution fusion | flops 1088684032 | bytes 13255680 | tf_op jit(solution)/shard_map/while/body/eval_jaxpr/cond/branch_1_fun/ngqk,knd->qngd/dot_general | solution.py:97
  185.4 5.6 %fusion.29 = f32[4,1024,128,1]{1,2,3,0:T(8,128)S(1)} fusion(bf16[128,4,4,128]{0,3,2,1:T(8,128)(2,1)} %get-tuple-element.627, f32[4,1024,128,4]{2,1,3,0:T(8,128)} %fusion.43, f32[4,4,128]{2,1,0:T(4,128)S(1)} %get-tuple-element.625, pred[128,1024]{0,1:T(8,128)(4,1)S(1)} %compare_and_fusion.1), kind=kOutput, calls=%fused_computation.33 | convolution fusion | flops 547356672 | bytes 11149312 | tf_op jit(solution)/shard_map/while/body/eval_jaxpr/cond/branch_1_fun/ngqk,qngd->knd/dot_general | solution.py:105
  191.1 1.3 copy-done.1
  192.4 1.9 copy.91
  194.3 1.5 constant_dynamic-update-slice_fusion.2
  195.9 70.1 %reduce-scatter.2.cloned.1.call-done = f32[128,512]{1,0:T(8,128)} async-done(((f32[2048,512]{1,0:T(8,128)}), f32[128,512]{1,0:T(8,128)}) %reduce-scatter.2.cloned.1.call-update) | async-done | bytes 262160 | tf_op jit(solution)/shard_map/reduce_scatter | solution.py:127
  265.9 5.6 %convolution_bitcast_fusion = f32[4096,512]{0,1:T(8,128)} fusion(bf16[128,4096]{1,0:T(8,128)(2,1)S(1)} %copy-done, f32[128,512]{1,0:T(8,128)} %reduce-scatter.2.cloned.1.call-done), kind=kOutput, calls=%fused_computation.60 | convolution fusion | flops 536936448 | bytes 9699328 | tf_op jit(solution)/shard_map/dot_general | solution.py:134
  271.6 184.4 %all-reduce.1 = bf16[4096,512]{0,1:T(8,128)(2,1)} all-reduce(f32[4096,512]{0,1:T(8,128)} %convolution_bitcast_fusion), channel_id=1, replica_groups=mesh['ctx'=16,'tp'=2] {'ctx'}, use_global_device_ids=true, to_apply=%region_11.12 | all-reduce | flops 2097152 | bytes 12582912 | tf_op jit(solution)/shard_map/psum | solution.py:135
  456.0 4.8 copy.89
  460.8 5.6 %all-to-all-start = ((bf16[2,2048,512]{1,2,0:T(8,128)(2,1)}), bf16[2,2048,512]{1,2,0:T(8,128)(2,1)}, u32[]{:S(2)}, u32[]{:S(2)}) async-start(bf16[2,2048,512]{1,2,0:T(8,128)(2,1)} %bitcast.130), calls=%async_computation.1 | async-start | bytes 8388608 | tf_op jit(solution)/shard_map/all_to_all | solution.py:137
  466.4 1.4 multiply_convert_fusion
  467.8 1.0 copy.84
  468.8 44.2 %all-to-all-done = bf16[2,2048,512]{1,2,0:T(8,128)(2,1)} async-done(((bf16[2,2048,512]{1,2,0:T(8,128)(2,1)}), bf16[2,2048,512]{1,2,0:T(8,128)(2,1)}, u32[]{:S(2)}, u32[]{:S(2)}) %all-to-all-start) | async-done | bytes 4194336 | tf_op jit(solution)/shard_map/all_to_all | solution.py:137
  513.0 6.7 %convert_multiply_fusion = f32[2,2048,512]{1,2,0:T(8,128)} fusion(bf16[2,2048,512]{1,2,0:T(8,128)(2,1)} %all-to-all-done), kind=kLoop, calls=%fused_computation.59 | loop fusion | flops 4194304 | bytes 12582912 | tf_op jit(solution)/shard_map/mul | solution.py:137
  519.6 9.2 %copy.65 = f32[2048,1024]{1,0:T(8,128)} copy(f32[2048,1024]{0,1:T(8,128)} %bitcast.128) | data formatting | bytes 16777216
  (60 shorter events, 8.8 us)
Async XLA Ops:
  7.2 258.8 %copy-start = (bf16[128,4096]{1,0:T(8,128)(2,1)S(1)}, bf16[128,4096]{1,0:T(8,128)(2,1)}, u32[]{:S(2)}) copy-start(bf16[128,4096]{1,0:T(8,128)(2,1)} %param.18) | copy-start | bytes 3145732
  7.2 91.5 %copy-start.4 = (s32[2048]{0:T(1024)S(1)}, s32[2048]{0:T(1024)}, u32[]{:S(2)}) copy-start(s32[2048]{0:T(1024)} %param.19) | copy-start | bytes 24580
  7.2 45.1 %all-gather.3.cloned.1.call-start = ((), (), s32[]{:S(2)}) async-start(), calls=%async_computation.2 | async-start | bytes 2228224 | tf_op jit(solution)/shard_map/all_gather | solution.py:21
  9.0 85.6 %all-gather.5.cloned.1.call-start = ((), (), s32[]{:S(2)}) async-start(), calls=%async_computation.3 | async-start | bytes 2228224 | tf_op jit(solution)/shard_map/all_gather | solution.py:22
  10.7 255.2 %reduce-scatter.2.cloned.1.call-start = ((), (), s32[]{:S(2)}) async-start(), calls=%async_computation.4 | async-start | bytes 4456448 | tf_op jit(solution)/shard_map/reduce_scatter | solution.py:127
  105.6 5.0 copy-start.3
  120.6 5.0 copy-start.3
  135.6 9.1 %copy-start.2 = (bf16[128,4,4,128]{0,3,2,1:T(8,128)(2,1)S(1)}, bf16[128,4,4,128]{0,3,2,1:T(8,128)(2,1)}, u32[]{:S(2)}) copy-start(bf16[128,4,4,128]{0,3,2,1:T(8,128)(2,1)} %get-tuple-element.627) | copy-start | bytes 1572868 | tf_op jit(solution)/shard_map/while/body/eval_jaxpr/cond
  159.0 1.3 copy-start.1
  167.6 9.1 %copy-start.2 = (bf16[128,4,4,128]{0,3,2,1:T(8,128)(2,1)S(1)}, bf16[128,4,4,128]{0,3,2,1:T(8,128)(2,1)}, u32[]{:S(2)}) copy-start(bf16[128,4,4,128]{0,3,2,1:T(8,128)(2,1)} %get-tuple-element.627) | copy-start | bytes 1572868 | tf_op jit(solution)/shard_map/while/body/eval_jaxpr/cond
  191.1 1.3 copy-start.1
  460.8 52.2 %all-to-all-start = ((bf16[2,2048,512]{1,2,0:T(8,128)(2,1)}), bf16[2,2048,512]{1,2,0:T(8,128)(2,1)}, u32[]{:S(2)}, u32[]{:S(2)}) async-start(bf16[2,2048,512]{1,2,0:T(8,128)(2,1)} %bitcast.130), calls=%async_computation.1 | async-start | bytes 8388608 | tf_op jit(solution)/shard_map/all_to_all | solution.py:137
Sparse Core Ops, SparseCore 0:
  10.8 41.5 all-gather.2
  54.5 40.1 all-gather.4
  196.0 69.9 reduce-scatter.1
where the time goes:
time: 538 us; the launch traced here: 535 us
  waiting for transfers between devices  189 us (35%)
  blocking collectives  184 us (34%)
  matrix products  58.6 us (11%)
  local copies, waits for them, and re-layouts  47.7 us (9%)
  loops' own time  18.5 us (3%)
  other arithmetic  17.5 us (3%)
  between operations  13.9 us (3%)
  starting transfers between devices  5.72 us (1%)
    psum x1, blocking collectives, per_device(): summed = lax.psum(own_term, 'ctx')  184 us
    reduce_scatter x1, waiting for transfers between devices, per_device(): lax.psum_scatter(blocks.reshape(tokens, heads_kv * HD), 'ctx', scatter_di...  70.1 us
    all_to_all x1, waiting for transfers between devices, per_device(): lax.all_to_all(summed.astype(jnp.bfloat16), 'tp', split_axis=0, concat_ax...  44.2 us
    all_gather x1, waiting for transfers between devices, per_device(): lax.all_gather(values, 'ctx', axis=0, tiled=True)  38.4 us
    all_gather x1, waiting for transfers between devices, per_device(): lax.all_gather(keys, 'ctx', axis=0, tiled=True)  36.4 us
    unnamed x13, local copies, waits for them, and re-layouts  25.3 us
    dot_general x4, matrix products, masked_scores(): jnp.einsum('qngd,knd->ngqk', query_heads, key_block, preferred_element_ty...  17.9 us
    dot_general x2, matrix products, query_update(): jnp.einsum('ngqk,knd->qngd', dscore.astype(jnp.bfloat16), key_block, pref...  17.4 us
  transfers between devices with their start and end apart: 4, of which 4 were waited for; matrix products, arithmetic and copies ran while one was open for 2% of the time, Pallas kernels for 0%

commit v1 on v0

v1 whole, which is shorter than its diff:
```python
import functools
import math

import jax
import jax.numpy as jnp
from jax import lax
from jax.experimental import pallas as pl
from jax.experimental.pallas import tpu as pltpu
from jax.sharding import PartitionSpec as P

HD = 128
MESH = pl.DeviceIdType.MESH
BF16 = jnp.bfloat16
F32 = jnp.float32


def attention_kernel(
    span_ref, q_ref, do_ref, k_ref, v_ref, start_ref, pos_ref, dq_ref, vg_ref, s_ref, dp_ref, *, group, width
):
    rows = q_ref.shape[0]
    wide = group * rows
    nt = (((1,), (1,)), ((), ()))
    tn = (((0,), (0,)), ((), ()))
    coef = HD ** (-0.5) * math.log2(math.e)
    lo, hi = span_ref[0], span_ref[1]
    qs = jnp.concatenate([q_ref[:, g * HD : (g + 1) * HD] for g in range(group)], axis=0)
    ds = jnp.concatenate([do_ref[:, g * HD : (g + 1) * HD] for g in range(group)], axis=0)
    start, pos = start_ref[...], pos_ref[...]
    vg_ref[...] = jnp.zeros_like(vg_ref)

    def first(j, top):
        at = pl.ds(pl.multiple_of(j * width, width), width)
        s = lax.dot_general(k_ref[at, :], qs, nt, preferred_element_type=F32)
        kpos = j * width + lax.broadcasted_iota(jnp.int32, (width, wide), 0)
        s = jnp.where((kpos >= start) & (kpos <= pos), s * coef, -1e30)
        s_ref[at, :] = s
        return jnp.maximum(top, jnp.max(s, axis=0, keepdims=True))

    top = lax.fori_loop(lo, hi, first, jnp.full((1, wide), -1e30, F32))

    def second(j, carry):
        total, dsum = carry
        at = pl.ds(pl.multiple_of(j * width, width), width)
        dp = lax.dot_general(v_ref[at, :], ds, nt, preferred_element_type=F32)
        w = jnp.exp2(s_ref[at, :] - top)
        s_ref[at, :] = w
        dp_ref[at, :] = dp
        return (
            total + jnp.sum(w, axis=0, keepdims=True),
            dsum + jnp.sum(w * dp, axis=0, keepdims=True),
        )

    zero = jnp.zeros((1, wide), F32)
    total, dsum = lax.fori_loop(lo, hi, second, (zero, zero))
    inv = 1.0 / total
    delta = dsum * inv

    def third(j, acc):
        at = pl.ds(pl.multiple_of(j * width, width), width)
        p = s_ref[at, :] * inv
        g = p * (dp_ref[at, :] - delta)
        vg_ref[at, :] = jnp.dot(p.astype(BF16), ds, preferred_element_type=F32).astype(BF16)
        return acc + lax.dot_general(k_ref[at, :], g.astype(BF16), tn, preferred_element_type=F32)

    acc = lax.fori_loop(lo, hi, third, jnp.zeros((HD, wide), F32))
    dq = (acc * HD ** (-0.5)).T.astype(BF16)
    for g in range(group):
        dq_ref[:, g * HD : (g + 1) * HD] = dq[g * rows : (g + 1) * rows, :]


def attention(queries, out_grad, key_all, value_all, segment_ids, first):
    rows = queries.shape[0]
    tokens = segment_ids.shape[0]
    heads_kv = key_all.shape[1] // HD
    group = queries.shape[1] // HD // heads_kv
    width = math.gcd(tokens, 256)
    seg_own = lax.dynamic_slice_in_dim(segment_ids, first, rows, 0)
    start = jnp.sum((segment_ids[:, None] < seg_own[None, :]).astype(jnp.int32), axis=0)
    pos = first + jnp.arange(rows, dtype=jnp.int32)
    span = jnp.stack([start[0] // width, (first + rows + width - 1) // width])
    wide = group * rows
    column = lambda n, *_: (0, n)
    whole = lambda n, *_: (0, 0)
    return pl.pallas_call(
        functools.partial(attention_kernel, group=group, width=width),
        out_shape=(
            jax.ShapeDtypeStruct(queries.shape, BF16),
            jax.ShapeDtypeStruct(key_all.shape, BF16),
        ),
        grid_spec=pltpu.PrefetchScalarGridSpec(
            num_scalar_prefetch=1,
            grid=(heads_kv,),
            in_specs=[
                pl.BlockSpec((rows, group * HD), column),
                pl.BlockSpec((rows, group * HD), column),
                pl.BlockSpec((tokens, HD), column),
                pl.BlockSpec((tokens, HD), column),
                pl.BlockSpec((1, wide), whole),
                pl.BlockSpec((1, wide), whole),
            ],
            out_specs=[
                pl.BlockSpec((rows, group * HD), column),
                pl.BlockSpec((tokens, HD), column),
            ],
            scratch_shapes=[pltpu.VMEM((tokens, wide), F32), pltpu.VMEM((tokens, wide), F32)],
        ),
        compiler_params=pltpu.CompilerParams(vmem_limit_bytes=48 << 20),
        cost_estimate=pl.CostEstimate(
            flops=8 * wide * tokens * HD * heads_kv,
            bytes_accessed=4 * (key_all.size + queries.size) * 2,
            transcendentals=wide * tokens * heads_kv,
        ),
        name="attention",
    )(
        span.astype(jnp.int32),
        queries,
        out_grad,
        key_all,
        value_all,
        jnp.tile(start, group)[None, :],
        jnp.tile(pos, group)[None, :],
    )


class Place:
    def __init__(self, n):
        self.A, self.B, self.C = n // 4, 2, 2
        self.me = lax.axis_index("ctx")
        self.a = self.me // (self.B * self.C)
        self.b = lax.rem(self.me // self.C, self.B)
        self.c = lax.rem(self.me, self.C)
        self.steps = sorted(range(1, self.A), key=lambda k: min(k, self.A - k))

    def at(self, da=0, db=0, dc=0):
        a = lax.rem(self.a + da + self.A, self.A)
        b = lax.rem(self.b + db + self.B, self.B)
        c = lax.rem(self.c + dc + self.C, self.C)
        return (a * self.B + b) * self.C + c


def greet(place, tp_peers=()):
    barrier = pltpu.get_barrier_semaphore()
    peers = [{"ctx": place.at(da=k)} for k in place.steps]
    peers += [{"ctx": place.at(db=1)}, {"ctx": place.at(dc=1)}]
    peers += [{"tp": p} for p in tp_peers]
    for peer in peers:
        pl.semaphore_signal(barrier, inc=1, device_id=peer, device_id_type=MESH)
    pl.semaphore_wait(barrier, len(peers))


class Gather:
    def __init__(self, place, src, out, send, recv):
        self.p, self.src, self.out, self.send, self.recv = place, src, out, send, recv
        self.sent = []

    def copy(self, src, slot, sem, target):
        return pltpu.make_async_remote_copy(
            src_ref=src,
            dst_ref=self.out.at[slot],
            send_sem=self.send.at[sem],
            recv_sem=self.recv.at[sem],
            device_id={"ctx": target},
            device_id_type=MESH,
        )

    def push(self, src, slot, sem, target):
        copy = self.copy(src, slot, sem, target)
        copy.start()
        self.sent.append(copy)

    def arrived(self, slot, sem):
        self.copy(self.out.at[slot], slot, sem, self.p.at(dc=1)).wait_recv()

    def begin(self):
        p = self.p
        for k in p.steps:
            self.push(self.src, p.me, k, p.at(da=k))
        self.push(self.src, p.me, p.A, p.at(db=1))
        self.push(self.src, p.me, 2 * p.A, p.at(dc=1))

    def along_a(self, k):
        p = self.p
        slot = p.at(da=-k)
        self.arrived(slot, k)
        self.push(self.out.at[slot], slot, p.A + k, p.at(db=1))
        self.push(self.out.at[slot], slot, 2 * p.A + k, p.at(dc=1))

    def along_b(self, k):
        p = self.p
        slot = p.at(da=-k, db=1)
        self.arrived(slot, p.A + k)
        self.push(self.out.at[slot], slot, 3 * p.A + k, p.at(dc=1))

    def finish(self):
        p = self.p
        for k in range(p.A):
            self.arrived(p.at(da=-k, dc=1), 2 * p.A + k)
            self.arrived(p.at(da=-k, db=1, dc=1), 3 * p.A + k)
        for copy in self.sent:
            copy.wait_send()


def run_gathers(gathers, begun=0):
    p = gathers[0].p
    for g in gathers[begun:]:
        g.begin()
    for k in p.steps:
        for g in gathers:
            g.along_a(k)
    for k in [0] + p.steps:
        for g in gathers:
            g.along_b(k)
    for g in gathers:
        g.finish()


def gather_kernel(n, count, *refs):
    srcs, outs = refs[:count], refs[count : 2 * count]
    send, recv, own = refs[2 * count :]
    place = Place(n)
    local = []
    for i in range(count):
        copy = pltpu.make_async_copy(srcs[i], outs[i].at[place.me], own.at[i])
        copy.start()
        local.append(copy)
    greet(place)
    run_gathers([Gather(place, srcs[i], outs[i], send.at[i], recv.at[i]) for i in range(count)])
    for copy in local:
        copy.wait()


def gather(arrays, n, collective_id):
    count = len(arrays)
    outs = pl.pallas_call(
        functools.partial(gather_kernel, n, count),
        out_shape=[jax.ShapeDtypeStruct((n,) + a.shape, a.dtype) for a in arrays],
        in_specs=[pl.BlockSpec(memory_space=pl.ANY)] * count,
        out_specs=[pl.BlockSpec(memory_space=pl.ANY)] * count,
        scratch_shapes=[
            pltpu.SemaphoreType.DMA((count, n)),
            pltpu.SemaphoreType.DMA((count, n)),
            pltpu.SemaphoreType.DMA((count,)),
        ],
        compiler_params=pltpu.CompilerParams(collective_id=collective_id, has_side_effects=True),
        name="gather%d" % collective_id,
    )(*arrays)
    return [o.reshape((n * a.shape[0],) + a.shape[1:]) for o, a in zip(outs, arrays)]


def reduce_kernel(n, parts, out, mine, one, sum_one, two, sum_two, three, send, recv, own):
    place = Place(n)
    A = place.A
    order = place.steps + [0]
    a_of = {k: lax.rem(place.a + k, A) for k in order}
    local = {}
    for k in order:
        local[k] = pltpu.make_async_copy(
            parts.at[a_of[k], :, place.c], mine.at[a_of[k]], own.at[k]
        )
        local[k].start()
    greet(place)

    def remote(src, dst, sem, target):
        return pltpu.make_async_remote_copy(
            src_ref=src,
            dst_ref=dst,
            send_sem=send.at[sem],
            recv_sem=recv.at[sem],
            device_id={"ctx": target},
            device_id_type=MESH,
        )

    sib, side = place.at(dc=1), place.at(db=1)
    started = []
    core, cross, line = {}, {}, {}
    for k in order:
        core[k] = remote(parts.at[a_of[k], :, 1 - place.c], one.at[a_of[k]], k, sib)
        core[k].start()
    for k in order:
        local[k].wait()
        core[k].wait_recv()
        at = a_of[k]
        sum_one[at] = (mine[at].astype(F32) + one[at].astype(F32)).astype(BF16)
        cross[k] = remote(sum_one.at[at, 1 - place.b], two.at[at], A + k, side)
        cross[k].start()
    for k in order:
        cross[k].wait_recv()
        at = a_of[k]
        sum_two[at] = (sum_one[at, place.b].astype(F32) + two[at].astype(F32)).astype(BF16)
        if k:
            line[k] = remote(sum_two.at[at], three.at[k], 2 * A + k, place.at(da=k))
            line[k].start()
    total = sum_two[place.a].astype(F32)
    for k in place.steps:
        line[k].wait_recv()
        total = total + three[k].astype(F32)
    out[...] = total.astype(BF16)
    for copies in (core, cross, line):
        for copy in copies.values():
            copy.wait_send()


def reduce(parts, n, collective_id):
    rows, cols = parts.shape[0] // n, parts.shape[1]
    A = n // 4
    block = lambda *lead: pltpu.VMEM(lead + (rows, cols), BF16)
    return pl.pallas_call(
        functools.partial(reduce_kernel, n),
        out_shape=jax.ShapeDtypeStruct((rows, cols), BF16),
        in_specs=[pl.BlockSpec(memory_space=pl.ANY)],
        out_specs=pl.BlockSpec(memory_space=pltpu.VMEM),
        scratch_shapes=[
            block(A, 2),
            block(A, 2),
            block(A, 2),
            block(A),
            block(A),
            block(A),
            pltpu.SemaphoreType.DMA((n,)),
            pltpu.SemaphoreType.DMA((n,)),
            pltpu.SemaphoreType.DMA((A,)),
        ],
        compiler_params=pltpu.CompilerParams(
            collective_id=collective_id, has_side_effects=True, vmem_limit_bytes=32 << 20
        ),
        name="reduce",
    )(parts.reshape(A, 2, 2, rows, cols))


def spread_kernel(n, tp, w, out, send, recv, own, tp_send, tp_recv):
    place = Place(n)
    t = lax.axis_index("tp")
    local = pltpu.make_async_copy(w.at[t], out.at[t, place.me], own)
    local.start()
    others = [lax.rem(t + k, tp) for k in range(1, tp)]
    greet(place, others)
    copies = []
    for k in range(1, tp):
        copy = pltpu.make_async_remote_copy(
            src_ref=w.at[others[k - 1]],
            dst_ref=out.at[t, place.me],
            send_sem=tp_send.at[k],
            recv_sem=tp_recv.at[k],
            device_id={"tp": others[k - 1]},
            device_id_type=MESH,
        )
        copy.start()
        copies.append(copy)
    gathers = [Gather(place, w.at[t], out.at[t], send.at[0], recv.at[0])]
    gathers[0].begin()
    for k in range(1, tp):
        source = lax.rem(t - k + tp, tp)
        copies[k - 1].wait_recv()
        more = Gather(place, out.at[source, place.me], out.at[source], send.at[k], recv.at[k])
        more.begin()
        gathers.append(more)
    run_gathers(gathers, len(gathers))
    for copy in copies:
        copy.wait_send()
    local.wait()


def spread(w, n, tp, collective_id):
    return pl.pallas_call(
        functools.partial(spread_kernel, n, tp),
        out_shape=jax.ShapeDtypeStruct((tp, n) + w.shape[1:], BF16),
        in_specs=[pl.BlockSpec(memory_space=pl.ANY)],
        out_specs=pl.BlockSpec(memory_space=pl.ANY),
        scratch_shapes=[
            pltpu.SemaphoreType.DMA((tp, n)),
            pltpu.SemaphoreType.DMA((tp, n)),
            pltpu.SemaphoreType.DMA,
            pltpu.SemaphoreType.DMA((tp,)),
            pltpu.SemaphoreType.DMA((tp,)),
        ],
        compiler_params=pltpu.CompilerParams(collective_id=collective_id, has_side_effects=True),
        name="spread",
    )(w)


def widen_kernel(w_ref, out_ref):
    slots, rows, cols = w_ref.shape[1:]
    for i in range(w_ref.shape[0]):
        for j in range(slots):
            out_ref[j * rows : (j + 1) * rows, i * cols : (i + 1) * cols] = w_ref[i, j].astype(F32)


def widen(w):
    tp, n, rows, cols = w.shape
    slots = 2
    return pl.pallas_call(
        widen_kernel,
        out_shape=jax.ShapeDtypeStruct((n * rows, tp * cols), F32),
        grid=(n // slots,),
        in_specs=[pl.BlockSpec((tp, slots, rows, cols), lambda i: (0, i, 0, 0))],
        out_specs=pl.BlockSpec((slots * rows, tp * cols), lambda i: (i, 0)),
        compiler_params=pltpu.CompilerParams(vmem_limit_bytes=32 << 20),
        name="widen",
    )(w)


def per_device(n, tp, queries, keys, values, out_grad, features, segment_ids):
    rows = queries.shape[0]
    tokens = segment_ids.shape[0]
    inputs = features.shape[1]
    first = lax.axis_index("ctx") * rows
    factor = 1.0 / math.sqrt(tokens)
    contract = (((0,), (0,)), ((), ()))
    block = inputs // (n * tp)
    if n % 4 == 0 and rows % 16 == 0 and inputs % (n * tp) == 0 and block % 16 == 0:
        key_all, value_all = gather([keys, values], n, 0)
        cut = features.reshape(rows, tp, n, block).transpose(2, 0, 1, 3)
        own = lax.all_to_all(cut, "ctx", split_axis=0, concat_axis=0, tiled=True)
        own = own.reshape(tokens, tp * block)
        query_grads, parts = attention(queries, out_grad, key_all, value_all, segment_ids, first)
        value_b = reduce(parts, n, 1)
        (value_full,) = gather([value_b], n, 2)
        w = lax.dot_general(own, value_full, contract, preferred_element_type=F32) * factor
        w = w.astype(BF16).reshape(tp, block, -1)
        return query_grads, widen(spread(w, n, tp, 3))
    key_all = lax.all_gather(keys, "ctx", axis=0, tiled=True)
    value_all = lax.all_gather(values, "ctx", axis=0, tiled=True)
    query_grads, parts = attention(queries, out_grad, key_all, value_all, segment_ids, first)
    value_b = lax.psum_scatter(parts.astype(F32), "ctx", scatter_dimension=0, tiled=True).astype(BF16)
    term = lax.dot_general(features, value_b, contract, preferred_element_type=F32)
    summed = lax.psum(term, "ctx")
    weight_grad = lax.all_to_all(
        summed.astype(BF16), "tp", split_axis=0, concat_axis=1, tiled=True
    ).astype(F32)
    return query_grads, weight_grad * factor


def solution(mesh):
    placed = (P("ctx", "tp"), P("ctx", "tp"), P("ctx", "tp"), P("ctx", "tp"), P("ctx", None), P())
    return jax.shard_map(
        functools.partial(per_device, mesh.shape["ctx"], mesh.shape["tp"]),
        mesh=mesh,
        in_specs=placed,
        out_specs=(P("ctx", "tp"), P("tp", None)),
        check_vma=False,
    )
```

time: 538 us -> 190 us (0.35)
  waiting for transfers between devices: 189 us -> 0.01 us
  blocking collectives: 184 us -> 0 us
  Pallas kernels: 0 us -> 173 us
  matrix products: 58.6 us -> 1.43 us
  local copies, waits for them, and re-layouts: 47.7 us -> 8.75 us
  loops' own time: 18.5 us -> 0 us
  other arithmetic: 17.5 us -> 0.43 us
  between operations: 13.9 us -> 0.93 us
    psum x1 -> x0, blocking collectives: 184 us -> none  [per_device(): summed = lax.psum(own_term, 'ctx')]
    pallas_call x0 -> x6, Pallas kernels: none -> 173 us  [the longest x2 83.1 us: gather(): pl.pallas_call(functools.partial(gather_kernel, n, count), out_shape=[jax...]
    all_gather x2 -> x0, waiting for transfers between devices: 74.7 us -> none  [the longest x1 38.4 us: per_device(): lax.all_gather(values, 'ctx', axis=0, tiled=True)]
    reduce_scatter x1 -> x0, waiting for transfers between devices: 70.1 us -> none  [per_device(): lax.psum_scatter(blocks.reshape(tokens, heads_kv * HD), 'ctx', scatter_di...]
    dot_general x11 -> x1, matrix products: 58.6 us -> 1.43 us  [per_device(): lax.dot_general(own, value_full, contract, preferred_element_type=F32)]
    all_to_all x1, waiting for transfers between devices: 44.2 us -> 0.01 us  [per_device(): own = lax.all_to_all(cut, 'ctx', split_axis=0, concat_axis=0, tiled=True)]
    another operation x6 -> x0, loops' own time: 18.5 us -> none  [the longest x1 5.23 us: per_device(): (top, total, accum), _ = lax.scan(forward_step, initial, starts)]
    unnamed x13 -> x15, local copies, waits for them, and re-layouts: 25.3 us -> 6.94 us
  transfers between devices with their start and end apart: 4 -> 1, of which waited for: 4 -> 0; matrix products, arithmetic and copies ran while one was open for 2% -> 0% of each run, Pallas kernels for 0% -> 65%
where the time goes in v1:
time: 190 us; the launch traced here: 191 us
  Pallas kernels  173 us (91%)
  local copies, waits for them, and re-layouts  8.75 us (5%)
  starting transfers between devices  6.47 us (3%)
    pallas_call x2, Pallas kernels, gather(): pl.pallas_call(functools.partial(gather_kernel, n, count), out_shape=[jax...  83.1 us
    pallas_call x1, Pallas kernels, spread(): pl.pallas_call(functools.partial(spread_kernel, n, tp), out_shape=jax.Sha...  43.8 us
    pallas_call x1, Pallas kernels, reduce(): pl.pallas_call(functools.partial(reduce_kernel, n), out_shape=jax.ShapeDt...  22 us
    pallas_call x1, Pallas kernels, attention(): pl.pallas_call(functools.partial(attention_kernel, group=group, width=wid...  19.7 us
    unnamed x15, local copies, waits for them, and re-layouts  6.94 us
    all_to_all x1, starting transfers between devices, per_device(): own = lax.all_to_all(cut, 'ctx', split_axis=0, concat_axis=0, tiled=True)  6.47 us
    pallas_call x1, Pallas kernels, widen(): pl.pallas_call(widen_kernel, out_shape=jax.ShapeDtypeStruct((n * rows, tp...  4.66 us
  transfers between devices with their start and end apart: 1, of which 0 were waited for; matrix products, arithmetic and copies ran while one was open for 0% of the time, Pallas kernels for 65%

profile of v1, /device:TPU:17, one launch (start us, length us, event | category | flops | bytes accessed | tf_op | source)
XLA Modules:
  0.0 191.3 jit_solution(6732663092142524794)
XLA Ops:
  0.6 1.6 copy.13
  2.3 0.0 copy-start.6
  2.3 0.0 copy-start.3
  2.3 0.0 copy-start.4
  2.3 1.0 copy.14
  3.3 6.5 %all-to-all-start = ((bf16[16,128,2,128]{1,3,2,0:T(8,128)(2,1)}), bf16[16,128,2,128]{1,3,2,0:T(8,128)(2,1)S(1)}, u32[]{:S(2)}, u32[]{:S(2)}) async-start(bf16[16,128,2,128]{1,3,2,0:T(8,128)(2,1)} %copy.14), calls=%async_computation | async-start | bytes 2097152 | tf_op jit(solution)/shard_map/all_to_all | solution.py:413
  9.8 0.0 copy-done.6
  9.8 0.1 dynamic_slice.3
  9.9 0.4 convert_reduce_fusion
  10.4 62.0 %gather0.1 = (bf16[16,128,512]{2,1,0:T(8,128)(2,1)}, bf16[16,128,512]{2,1,0:T(8,128)(2,1)}) custom-call(bf16[128,512]{1,0:T(8,128)(2,1)} %refs_0_.1, bf16[128,512]{1,0:T(8,128)(2,1)} %refs_1_.1), custom_call_target="tpu_custom_call" | custom-call | tf_op jit(solution)/shard_map/gather0/pallas_call | solution.py:234
  72.4 0.1 pad_add_fusion.span_ref
  72.5 0.0 copy-done.3
  72.5 0.0 copy-done.4
  72.5 0.0 copy-start.2
  72.5 1.6 copy-done.2
  74.1 19.7 %attention.1 = (bf16[128,2048]{1,0:T(8,128)(2,1)}, bf16[2048,512]{1,0:T(8,128)(2,1)S(1)}) custom-call(s32[2]{0:T(128)S(1)} %pad_add_fusion.span_ref, bf16[128,2048]{1,0:T(8,128)(2,1)S(1)} %copy-done.3, bf16[128,2048]{1,0:T(8,128)(2,1)S(1)} %copy-done.4, bf16[2048,512]{1,0:T(8,128)(2,1)S(1)} %bitcast.27, bf16[2048,512]{1,0:T(8,128)(2,1)} %bitcast.36, ...), custom_call_target="tpu_custom_call" | custom-call | flops 4294967296 | bytes 10485760 | tf_op jit(solution)/shard_map/attention/pallas_call | solution.py:84
  93.8 22.0 %reduce.1.refs_0_ = bf16[128,512]{1,0:T(8,128)(2,1)S(1)} custom-call(bf16[4,2,2,128,512]{4,3,2,1,0:T(8,128)(2,1)S(1)} %bitcast.24), custom_call_target="tpu_custom_call" | custom-call | tf_op jit(solution)/shard_map/reduce/pallas_call | solution.py:307
  115.8 0.0 copy-start.1
  115.8 0.6 copy-done.1
  116.5 21.1 %gather2.1 = bf16[16,128,512]{2,1,0:T(8,128)(2,1)} custom-call(bf16[128,512]{1,0:T(8,128)(2,1)} %copy-done.1), custom_call_target="tpu_custom_call" | custom-call | tf_op jit(solution)/shard_map/gather2/pallas_call | solution.py:234
  137.6 0.0 all-to-all-done
  137.6 0.0 copy-start.5
  137.6 0.7 copy.15
  138.3 0.9 copy-done.5
  139.2 1.4 fusion
  140.6 43.8 %spread.1.w_ref = bf16[2,16,128,512]{3,2,1,0:T(8,128)(2,1)} custom-call(bf16[2,128,512]{2,1,0:T(8,128)(2,1)} %bitcast.31), custom_call_target="tpu_custom_call" | custom-call | tf_op jit(solution)/shard_map/spread/pallas_call | solution.py:364
  184.5 0.0 copy-start
  184.5 2.2 %copy-done = bf16[2,16,128,512]{3,2,1,0:T(8,128)(2,1)S(1)} copy-done((bf16[2,16,128,512]{3,2,1,0:T(8,128)(2,1)S(1)}, bf16[2,16,128,512]{3,2,1,0:T(8,128)(2,1)}, u32[]{:S(2)}) %copy-start) | copy-done | bytes 4194328
  186.6 4.7 %widen.1 = f32[2048,1024]{1,0:T(8,128)} custom-call(bf16[2,16,128,512]{3,2,1,0:T(8,128)(2,1)S(1)} %copy-done), custom_call_target="tpu_custom_call" | custom-call | tf_op jit(solution)/shard_map/widen/pallas_call | solution.py:391
  (3 shorter events, 0.0 us)
Async XLA Ops:
  2.3 7.6 %copy-start.6 = (s32[2048]{0:T(1024)S(1)}, s32[2048]{0:T(1024)}, u32[]{:S(2)}) copy-start(s32[2048]{0:T(1024)} %param.11) | copy-start | bytes 24580
  2.3 70.2 %copy-start.3 = (bf16[128,2048]{1,0:T(8,128)(2,1)S(1)}, bf16[128,2048]{1,0:T(8,128)(2,1)}, u32[]{:S(2)}) copy-start(bf16[128,2048]{1,0:T(8,128)(2,1)} %q_ref.1) | copy-start | bytes 1572868
  2.3 70.2 %copy-start.4 = (bf16[128,2048]{1,0:T(8,128)(2,1)S(1)}, bf16[128,2048]{1,0:T(8,128)(2,1)}, u32[]{:S(2)}) copy-start(bf16[128,2048]{1,0:T(8,128)(2,1)} %do_ref.1) | copy-start | bytes 1572868
  3.3 134.2 %all-to-all-start = ((bf16[16,128,2,128]{1,3,2,0:T(8,128)(2,1)}), bf16[16,128,2,128]{1,3,2,0:T(8,128)(2,1)S(1)}, u32[]{:S(2)}, u32[]{:S(2)}) async-start(bf16[16,128,2,128]{1,3,2,0:T(8,128)(2,1)} %copy.14), calls=%async_computation | async-start | bytes 2097152 | tf_op jit(solution)/shard_map/all_to_all | solution.py:413
  72.5 1.6 copy-start.2
  115.8 0.7 copy-start.1
  137.6 1.6 copy-start.5
  184.5 2.2 %copy-start = (bf16[2,16,128,512]{3,2,1,0:T(8,128)(2,1)S(1)}, bf16[2,16,128,512]{3,2,1,0:T(8,128)(2,1)}, u32[]{:S(2)}) copy-start(bf16[2,16,128,512]{3,2,1,0:T(8,128)(2,1)} %spread.1.w_ref) | copy-start | bytes 12582916
